TPU v7x, 32 devices: a whole 2x2x4 slice. The times are simulated.
32 devices in a mesh: quad: 16 (over z, x, core), rows: 2 (over y).
Axes of the slice: x: 2, y: 2, z: 4, core: 2. Of those that a mesh axis runs over, the one named last changes fastest.
Arguments:
- solutions: bfloat16 [32, 2, 64, 16, 1280], P('quad', None, None, None, 'rows'), may hold values from -64 to 64
- angles: float32 [32], replicated, may hold values from -3.140625 to 3.140625
- qweights: float32 [2, 32], replicated, may hold values from -1 to 1
- neighbours: int32 [320, 8], P(('quad', 'rows')), may hold values from 0 to 319, as said below
- hblocks: bfloat16 [320, 64, 512], P(('quad', 'rows')), may hold values from -0.25 to 0.25
Outputs:
- h_moments: bfloat16 [1024, 20480], P(None, ('quad', 'rows'))
- ritz_matrices: float32 [512, 2, 2, 512], P('quad')
Inputs may be any that keep to these rules, and one draw needn't show every extreme that they name: neighbours[c, 0] = c, neighbours[c, 1] = min(c + 2, 319), neighbours[c, 2] = max(c - 2, 0); every entry lies within 2 of c.
All inputs are finite; a program needn't handle non-finite values.
Results may differ from a plain program's by a relative error of at most 0.0075.
Values may be sent and summed in bfloat16 or wider, within the bound.
A program may use at most 64 MiB of HBM per device.

v0:
```python
import jax
import jax.numpy as jnp
from jax import lax
from jax.sharding import PartitionSpec as P

LCOL = 64
QPTS = 32
KMOM = 8
NB = 8
HALO = 2


def extended(block, sides, width):
    for axis, dim in sides:
        count = lax.axis_size(axis)
        forward = [(i, i + 1) for i in range(count - 1)]
        backward = [(target, source) for source, target in forward]
        low = lax.ppermute(
            lax.slice_in_dim(block, block.shape[dim] - width, None, axis=dim), axis, forward
        )
        high = lax.ppermute(lax.slice_in_dim(block, 0, width, axis=dim), axis, backward)
        block = jnp.concatenate([low, block, high], axis=dim)
    return block


def moment_coefficients(angles, qweights):
    order = jnp.arange(KMOM, dtype=jnp.float32)[:, None]
    phase = order * angles[None, :]
    cosine = jnp.cos(phase)
    sine = jnp.sin(phase)
    real_coef = qweights[0][None, :] * cosine - qweights[1][None, :] * sine
    imag_coef = qweights[0][None, :] * sine + qweights[1][None, :] * cosine
    real_rows = jnp.stack([real_coef, -imag_coef], -1)
    imag_rows = jnp.stack([imag_coef, real_coef], -1)
    mixing = jnp.stack([real_rows, imag_rows], 0)
    return mixing.reshape(2 * KMOM, 2 * QPTS).astype(jnp.bfloat16)


def split_parts(product, half_cols, row_count):
    real_part = product[:row_count, :half_cols] + product[row_count:, half_cols:]
    imag_part = product[:row_count, half_cols:] - product[row_count:, :half_cols]
    return jnp.stack([real_part, imag_part], 1)


def gram_part(moments, applied, first_row, row_count, total_rows):
    half_cols = moments.shape[0] // 2
    chosen = jnp.concatenate(
        [
            lax.dynamic_slice_in_dim(moments, first_row, row_count, 0),
            lax.dynamic_slice_in_dim(moments, half_cols + first_row, row_count, 0),
        ],
        0,
    )
    contract = (((1,), (1,)), ((), ()))
    plain = lax.dot_general(chosen, moments, contract, preferred_element_type=jnp.float32)
    mixed = lax.dot_general(chosen, applied, contract, preferred_element_type=jnp.float32)
    ritz = jnp.stack(
        [split_parts(plain, half_cols, row_count), split_parts(mixed, half_cols, row_count)], 1
    )
    return ritz * (1.0 / total_rows)


def per_device(solutions, angles, qweights, neighbours, hblocks):
    groups = lax.axis_size("quad") * lax.axis_size("rows")
    rows_dev = solutions.shape[4]
    cells_dev = hblocks.shape[0]
    orbitals = hblocks.shape[1]
    half_cols = KMOM * LCOL
    mixing = moment_coefficients(angles, qweights)
    received = lax.all_to_all(solutions, "quad", split_axis=3, concat_axis=0, tiled=True)
    stacked = received.reshape(QPTS * 2, LCOL, received.shape[4])
    result = jnp.einsum("pq,qln->pln", mixing, stacked, preferred_element_type=jnp.float32)
    moments = result.reshape(2 * half_cols, received.shape[4]).astype(jnp.bfloat16)
    padded = extended(moments, ((("quad", "rows"), 1),), HALO * orbitals)
    first_cell = (
        lax.axis_index("quad") * lax.axis_size("rows") + lax.axis_index("rows")
    ) * cells_dev
    local_index = (neighbours - first_cell + HALO).reshape(-1)
    cellwise = padded.reshape(2 * half_cols, cells_dev + 2 * HALO, orbitals)
    nearby = jnp.take(cellwise, local_index, axis=1).reshape(
        2 * half_cols, cells_dev, NB * orbitals
    )
    applied = jnp.einsum("cam,xcm->xca", hblocks, nearby, preferred_element_type=jnp.float32)
    applied = applied.reshape(2 * half_cols, rows_dev).astype(jnp.bfloat16)
    total_rows = rows_dev * groups
    share_rows = half_cols // lax.axis_size("quad")
    summed = lax.psum(gram_part(moments, applied, 0, half_cols, total_rows), ("quad", "rows"))
    ritz_matrices = lax.dynamic_slice_in_dim(
        summed, lax.axis_index("quad") * share_rows, share_rows, 0
    )
    return (applied, ritz_matrices)


def solution(mesh):
    in_specs = (
        P("quad", None, None, None, "rows"),
        P(),
        P(),
        P(("quad", "rows"), None),
        P(("quad", "rows"), None, None),
    )
    out_specs = (P(None, ("quad", "rows")), P("quad", None, None, None))
    return jax.shard_map(
        per_device, mesh=mesh, in_specs=in_specs, out_specs=out_specs, check_vma=False
    )
```

profile of v0, /device:TPU:0, one launch (start us, length us, event | category | flops | bytes accessed | tf_op | source)
XLA Modules:
  0.0 333.4 jit_solution(11366127904357081607)
XLA Ops:
  7.2 0.0 copy-start
  7.2 6.2 %copy.34 = bf16[2,2,64,16,640]{4,2,1,0,3:T(8,128)(2,1)} copy(bf16[2,2,64,16,640]{4,3,2,1,0:T(8,128)(2,1)} %param.5) | data formatting | bytes 10485760 | tf_op args[0]
  13.3 0.0 copy-start.5
  13.3 0.0 copy-start.6
  13.3 0.0 copy-start.4
  13.3 7.5 %all-to-all-start = ((bf16[2,2,64,16,640]{4,2,1,0,3:T(8,128)(2,1)}), bf16[2,2,64,16,640]{4,2,1,0,3:T(8,128)(2,1)}, u32[]{:S(2)}, u32[]{:S(2)}) async-start(bf16[2,2,64,16,640]{4,2,1,0,3:T(8,128)(2,1)} %copy.34), calls=%async_computation | async-start | bytes 10485760 | tf_op jit(solution)/shard_map/all_to_all | solution.py:70
  20.9 0.0 all-reduce.2.cloned.1.call-start
  20.9 0.0 copy-done.5
  21.0 0.0 copy-done.6
  21.0 0.1 negate_convert_fusion
  21.0 0.1 copy.33
  21.2 0.1 convert_element_type.30
  21.3 0.0 copy-done.4
  21.3 0.1 copy.39
  21.4 0.1 reshape.334
  21.5 0.1 copy.32
  21.6 0.1 broadcast_in_dim.16
  21.6 0.1 broadcast_in_dim.17
  21.8 95.1 %all-to-all-done = bf16[2,2,64,16,640]{4,2,1,0,3:T(8,128)(2,1)} async-done(((bf16[2,2,64,16,640]{4,2,1,0,3:T(8,128)(2,1)}), bf16[2,2,64,16,640]{4,2,1,0,3:T(8,128)(2,1)}, u32[]{:S(2)}, u32[]{:S(2)}) %all-to-all-start) | async-done | bytes 5242912 | tf_op jit(solution)/shard_map/all_to_all | solution.py:70
  116.8 6.5 %fusion.6 = bf16[16,64,640]{2,0,1:T(8,128)(2,1)S(1)} fusion(bf16[64,64,640]{2,1,0:T(8,128)(2,1)} %bitcast.7, bf16[16,64]{0,1:T(8,128)(2,1)S(1)} %convert_element_type.30), kind=kOutput, calls=%fused_computation.11 | convolution fusion | flops 84541440 | bytes 6555648 | tf_op jit(solution)/shard_map/pq,qln->pln/dot_general | solution.py:72
  123.3 0.3 copy.37
  123.6 0.0 copy-start.1
  123.7 1.8 fusion.23
  125.5 3.4 %collective-permute-start = (bf16[1024,128]{1,0:T(8,128)(2,1)S(1)}, bf16[1024,128]{1,0:T(8,128)(2,1)S(1)}, u32[]{:S(2)}, u32[]{:S(2)}) collective-permute-start(bf16[1024,128]{1,0:T(8,128)(2,1)S(1)} %get-tuple-element.14), channel_id=1, source_target_pairs={{0,1},{1,2},{2,3},{3,4},{4,5},{5,6},{6,7},{7,8},{8,9},{9,10},{10,1... | collective-permute-start | bytes 786440 | tf_op jit(solution)/shard_map/ppermute | solution.py:18
  128.9 1.5 collective-permute-start.1
  130.4 1.5 fusion.15
  131.9 3.7 %collective-permute-done = bf16[1024,128]{1,0:T(8,128)(2,1)S(1)} collective-permute-done((bf16[1024,128]{1,0:T(8,128)(2,1)S(1)}, bf16[1024,128]{1,0:T(8,128)(2,1)S(1)}, u32[]{:S(2)}, u32[]{:S(2)}) %collective-permute-start) | collective-permute-done | bytes 262176 | tf_op jit(solution)/shard_map/ppermute | solution.py:18
  135.6 1.6 collective-permute-done.1
  137.2 0.0 copy-done.1
  137.2 1.4 pad_maximum_fusion
  138.6 2.9 copy.38
  141.5 6.3 %gather_fusion = bf16[80,1024,64]{1,2,0:T(8,128)(2,1)} fusion(bf16[1024,14,64]{0,2,1:T(8,128)(2,1)S(1)} %bitcast.45, s32[1024]{0:T(1024)S(1)} %pad_clamp_fusion), kind=kCustom, calls=%fused_computation | custom fusion | bytes 20971840 | tf_op jit(solution)/shard_map/jit(_take)/gather | solution.py:80
  147.8 0.0 copy-done
  147.8 0.0 copy-start.2
  147.8 5.5 %fusion.9 = bf16[10,1024,64]{1,2,0:T(8,128)(2,1)S(1)} fusion(bf16[10,64,512]{2,1,0:T(8,128)(2,1)S(1)} %copy-done, bf16[1024,10,512]{0,2,1:T(8,128)(2,1)} %bitcast.46, pred[10,512]{1,0:T(8,128)(4,1)S(1)} %broadcast_in_dim.17), kind=kOutput, calls=%fused_computation.12 | convolution fusion | flops 676986880 | bytes 12456960 | tf_op jit(solution)/shard_map/cam,xcm->xca/dot_general | solution.py:83
  153.4 0.0 copy-done.2
  153.4 1.8 fusion.24
  155.2 0.0 copy-start.3
  155.2 0.5 fusion.13
  155.7 0.7 copy-done.3
  156.4 0.4 maximum_bitcast_fusion
  156.9 2.7 maximum_multiply_fusion
  159.6 0.0 all-reduce.2.cloned.1.call-update
  159.6 1.4 copy.41
  161.1 163.6 %all-reduce.2.cloned.1.call-done = f32[512,2,2,512]{3,0,2,1:T(8,128)} async-done(((f32[512,2,2,512]{3,0,2,1:T(8,128)}), f32[512,2,2,512]{3,0,2,1:T(8,128)}) %all-reduce.2.cloned.1.call-update) | async-done | bytes 4194320 | tf_op jit(solution)/shard_map/psum | solution.py:87
  324.7 1.0 constant_dynamic-slice_fusion
  325.6 0.9 copy.42
  (8 shorter events, 0.1 us)
Async XLA Ops:
  7.2 140.7 %copy-start = (bf16[10,64,512]{2,1,0:T(8,128)(2,1)S(1)}, bf16[10,64,512]{2,1,0:T(8,128)(2,1)}, u32[]{:S(2)}) copy-start(bf16[10,64,512]{2,1,0:T(8,128)(2,1)} %param.9) | copy-start | bytes 1966084
  13.3 7.6 %copy-start.5 = (f32[2,32]{1,0:T(2,128)S(1)}, f32[2,32]{1,0:T(2,128)}, u32[]{:S(2)}) copy-start(f32[2,32]{1,0:T(2,128)} %param.7) | copy-start | bytes 772
  13.3 7.6 %copy-start.6 = (f32[32]{0:T(128)S(1)}, f32[32]{0:T(128)}, u32[]{:S(2)}) copy-start(f32[32]{0:T(128)} %param.6) | copy-start | bytes 388
  13.3 7.9 %copy-start.4 = (s32[10,8]{0,1:T(8,128)S(1)}, s32[10,8]{0,1:T(8,128)}, u32[]{:S(2)}) copy-start(s32[10,8]{0,1:T(8,128)} %param.8) | copy-start | bytes 964
  13.3 103.5 %all-to-all-start = ((bf16[2,2,64,16,640]{4,2,1,0,3:T(8,128)(2,1)}), bf16[2,2,64,16,640]{4,2,1,0,3:T(8,128)(2,1)}, u32[]{:S(2)}, u32[]{:S(2)}) async-start(bf16[2,2,64,16,640]{4,2,1,0,3:T(8,128)(2,1)} %copy.34), calls=%async_computation | async-start | bytes 10485760 | tf_op jit(solution)/shard_map/all_to_all | solution.py:70
  20.9 303.8 %all-reduce.2.cloned.1.call-start = ((), (), s32[]{:S(2)}) async-start(), calls=%async_computation.1 | async-start | bytes 8388608 | tf_op jit(solution)/shard_map/psum | solution.py:87
  123.6 13.6 %copy-start.1 = (bf16[16,64,640]{2,1,0:T(8,128)(2,1)}, bf16[16,64,640]{2,1,0:T(8,128)(2,1)S(1)}, u32[]{:S(2)}) copy-start(bf16[16,64,640]{2,1,0:T(8,128)(2,1)S(1)} %copy.37) | copy-start | bytes 3932164
  125.5 10.1 %collective-permute-start = (bf16[1024,128]{1,0:T(8,128)(2,1)S(1)}, bf16[1024,128]{1,0:T(8,128)(2,1)S(1)}, u32[]{:S(2)}, u32[]{:S(2)}) collective-permute-start(bf16[1024,128]{1,0:T(8,128)(2,1)S(1)} %get-tuple-element.14), channel_id=1, source_target_pairs={{0,1},{1,2},{2,3},{3,4},{4,5},{5,6},{6,7},{7,8},{8,9},{9,10},{10,1... | collective-permute-start | bytes 786440 | tf_op jit(solution)/shard_map/ppermute | solution.py:18
  128.9 8.3 %collective-permute-start.1 = (bf16[1024,128]{1,0:T(8,128)(2,1)S(1)}, bf16[1024,128]{1,0:T(8,128)(2,1)S(1)}, u32[]{:S(2)}, u32[]{:S(2)}) collective-permute-start(bf16[1024,128]{1,0:T(8,128)(2,1)S(1)} %get-tuple-element.15), channel_id=1, source_target_pairs={{1,0},{2,1},{3,2},{4,3},{5,4},{6,5},{7,6},{8,7},{9,8},{10,9},{11,1... | collective-permute-start | bytes 786440 | tf_op jit(solution)/shard_map/ppermute | solution.py:21
  147.8 5.6 %copy-start.2 = (bf16[16,64,640]{2,1,0:T(8,128)(2,1)S(1)}, bf16[16,64,640]{2,1,0:T(8,128)(2,1)}, u32[]{:S(2)}) copy-start(bf16[16,64,640]{2,1,0:T(8,128)(2,1)} %copy-done.1) | copy-start | bytes 3932164
  155.2 1.2 copy-start.3
Sparse Core Ops, SparseCore 0:
  159.7 164.8 all-reduce.1
where the time goes:
time: 334 us; the launch traced here: 333 us
  waiting for transfers between devices  264 us (79%)
  local copies, waits for them, and re-layouts  20.4 us (6%)
  matrix products  15.7 us (5%)
  between operations  14.2 us (4%)
  starting transfers between devices  12.5 us (4%)
  other arithmetic  6.65 us (2%)
    psum x1, waiting for transfers between devices, per_device(): lax.psum(gram_part(moments, applied, 0, half_cols, total_rows), ('quad',...  164 us
    all_to_all x1, waiting for transfers between devices, per_device(): lax.all_to_all(solutions, 'quad', split_axis=3, concat_axis=0, tiled=True)  95.1 us
    unnamed x17, local copies, waits for them, and re-layouts  9.26 us
    all_to_all x1, starting transfers between devices, per_device(): lax.all_to_all(solutions, 'quad', split_axis=3, concat_axis=0, tiled=True)  7.53 us
  transfers between devices with their start and end apart: 4, of which 4 were waited for; matrix products, arithmetic and copies ran while one was open for 1% of the time, Pallas kernels for 0%

commit v1 on v0

--- a/solution.py
+++ b/solution.py
@@ -84,7 +84,9 @@
     applied = applied.reshape(2 * half_cols, rows_dev).astype(jnp.bfloat16)
     total_rows = rows_dev * groups
     share_rows = half_cols // lax.axis_size("quad")
-    summed = lax.psum(gram_part(moments, applied, 0, half_cols, total_rows), ("quad", "rows"))
+    summed = lax.psum(
+        lax.psum(gram_part(moments, applied, 0, half_cols, total_rows), "rows"), "quad"
+    )
     ritz_matrices = lax.dynamic_slice_in_dim(
         summed, lax.axis_index("quad") * share_rows, share_rows, 0
     )

time: 334 us -> 416 us (1.25)
  waiting for transfers between devices: 264 us -> 346 us
    psum x1 -> x2, waiting for transfers between devices: 164 us -> 245 us  [the longest x1 131 us: per_device(): lax.psum(gram_part(moments, applied, 0, half_cols, total_rows), 'rows')]
  transfers between devices with their start and end apart: 4 -> 5, of which waited for: 4 -> 5; matrix products, arithmetic and copies ran while one was open for 1% -> 1% of each run, Pallas kernels for 0% -> 0%
where the time goes in v1:
time: 416 us; the launch traced here: 415 us
  waiting for transfers between devices  346 us (83%)
  local copies, waits for them, and re-layouts  20.4 us (5%)
  matrix products  15.7 us (4%)
  between operations  14.3 us (3%)
  starting transfers between devices  12.5 us (3%)
  other arithmetic  6.65 us (2%)
    psum x1, waiting for transfers between devices, per_device(): lax.psum(gram_part(moments, applied, 0, half_cols, total_rows), 'rows')  131 us
    psum x1, waiting for transfers between devices, per_device(): lax.psum(lax.psum(gram_part(moments, applied, 0, half_cols, total_rows),...  114 us
    all_to_all x1, waiting for transfers between devices, per_device(): lax.all_to_all(solutions, 'quad', split_axis=3, concat_axis=0, tiled=True)  95.1 us
    unnamed x17, local copies, waits for them, and re-layouts  9.26 us
  transfers between devices with their start and end apart: 5, of which 5 were waited for; matrix products, arithmetic and copies ran while one was open for 1% of the time, Pallas kernels for 0%

profile of v1, /device:TPU:0, one launch (start us, length us, event | category | flops | bytes accessed | tf_op | source)
XLA Modules:
  0.0 415.2 jit_solution(16583726541498872045)
XLA Ops:
  7.2 0.0 copy-start
  7.2 6.2 %copy.34 = bf16[2,2,64,16,640]{4,2,1,0,3:T(8,128)(2,1)} copy(bf16[2,2,64,16,640]{4,3,2,1,0:T(8,128)(2,1)} %param.5) | data formatting | bytes 10485760 | tf_op args[0]
  13.3 0.0 copy-start.5
  13.3 0.0 copy-start.6
  13.3 7.5 %all-to-all-start = ((bf16[2,2,64,16,640]{4,2,1,0,3:T(8,128)(2,1)}), bf16[2,2,64,16,640]{4,2,1,0,3:T(8,128)(2,1)}, u32[]{:S(2)}, u32[]{:S(2)}) async-start(bf16[2,2,64,16,640]{4,2,1,0,3:T(8,128)(2,1)} %copy.34), calls=%async_computation | async-start | bytes 10485760 | tf_op jit(solution)/shard_map/all_to_all | solution.py:70
  20.9 0.0 all-reduce.3.cloned.1.call-start
  20.9 0.0 copy-done.5
  21.0 0.0 copy-done.6
  21.0 0.1 negate_convert_fusion
  21.0 0.1 copy.33
  21.2 0.1 convert_element_type.30
  21.3 0.0 copy-done.4
  21.3 0.1 copy.39
  21.4 0.1 reshape.334
  21.5 0.1 copy.32
  21.6 0.1 broadcast_in_dim.16
  21.6 0.1 broadcast_in_dim.17
  21.8 95.1 %all-to-all-done = bf16[2,2,64,16,640]{4,2,1,0,3:T(8,128)(2,1)} async-done(((bf16[2,2,64,16,640]{4,2,1,0,3:T(8,128)(2,1)}), bf16[2,2,64,16,640]{4,2,1,0,3:T(8,128)(2,1)}, u32[]{:S(2)}, u32[]{:S(2)}) %all-to-all-start) | async-done | bytes 5242912 | tf_op jit(solution)/shard_map/all_to_all | solution.py:70
  116.8 6.5 %fusion.6 = bf16[16,64,640]{2,0,1:T(8,128)(2,1)S(1)} fusion(bf16[64,64,640]{2,1,0:T(8,128)(2,1)} %bitcast.7, bf16[16,64]{0,1:T(8,128)(2,1)S(1)} %convert_element_type.30), kind=kOutput, calls=%fused_computation.11 | convolution fusion | flops 84541440 | bytes 6555648 | tf_op jit(solution)/shard_map/pq,qln->pln/dot_general | solution.py:72
  123.3 0.3 copy.37
  123.6 0.0 copy-start.1
  123.7 1.8 fusion.23
  125.5 3.4 collective-permute-start
  128.9 1.5 collective-permute-start.1
  130.4 1.5 fusion.15
  131.9 3.7 collective-permute-done
  135.6 1.6 collective-permute-done.1
  137.2 0.0 copy-done.1
  137.2 1.4 pad_maximum_fusion
  138.6 2.9 copy.38
  141.5 6.3 %gather_fusion = bf16[80,1024,64]{1,2,0:T(8,128)(2,1)} fusion(bf16[1024,14,64]{0,2,1:T(8,128)(2,1)S(1)} %bitcast.45, s32[1024]{0:T(1024)S(1)} %pad_clamp_fusion), kind=kCustom, calls=%fused_computation | custom fusion | bytes 20971840 | tf_op jit(solution)/shard_map/jit(_take)/gather | solution.py:80
  147.8 0.0 copy-done
  147.8 5.5 %fusion.9 = bf16[10,1024,64]{1,2,0:T(8,128)(2,1)S(1)} fusion(bf16[10,64,512]{2,1,0:T(8,128)(2,1)S(1)} %copy-done, bf16[1024,10,512]{0,2,1:T(8,128)(2,1)} %bitcast.46, pred[10,512]{1,0:T(8,128)(4,1)S(1)} %broadcast_in_dim.17), kind=kOutput, calls=%fused_computation.12 | convolution fusion | flops 676986880 | bytes 12456960 | tf_op jit(solution)/shard_map/cam,xcm->xca/dot_general | solution.py:83
  153.4 0.0 copy-done.2
  153.4 1.8 fusion.24
  155.2 0.0 copy-start.3
  155.2 0.5 fusion.13
  155.7 0.7 copy-done.3
  156.4 0.4 maximum_bitcast_fusion
  156.9 2.7 maximum_multiply_fusion
  159.6 0.0 all-reduce.3.cloned.1.call-update
  159.6 0.0 all-reduce.5.cloned.1.call-start
  159.7 131.1 %all-reduce.3.cloned.1.call-done = f32[512,2,2,512]{3,0,2,1:T(8,128)} async-done(((f32[512,2,2,512]{3,0,2,1:T(8,128)}), f32[512,2,2,512]{3,0,2,1:T(8,128)}) %all-reduce.3.cloned.1.call-update) | async-done | bytes 4194320 | tf_op jit(solution)/shard_map/psum | solution.py:88
  290.8 0.0 all-reduce.5.cloned.1.call-update
  290.8 1.4 copy.41
  292.3 114.2 %all-reduce.5.cloned.1.call-done = f32[512,2,2,512]{3,0,2,1:T(8,128)} async-done(((f32[512,2,2,512]{3,0,2,1:T(8,128)}), f32[512,2,2,512]{3,0,2,1:T(8,128)}) %all-reduce.5.cloned.1.call-update) | async-done | bytes 4194320 | tf_op jit(solution)/shard_map/psum | solution.py:87
  406.4 1.0 constant_dynamic-slice_fusion
  407.4 0.9 copy.42
  (10 shorter events, 0.1 us)
Async XLA Ops:
  7.2 140.7 %copy-start = (bf16[10,64,512]{2,1,0:T(8,128)(2,1)S(1)}, bf16[10,64,512]{2,1,0:T(8,128)(2,1)}, u32[]{:S(2)}) copy-start(bf16[10,64,512]{2,1,0:T(8,128)(2,1)} %param.9) | copy-start | bytes 1966084
  13.3 7.6 %copy-start.5 = (f32[2,32]{1,0:T(2,128)S(1)}, f32[2,32]{1,0:T(2,128)}, u32[]{:S(2)}) copy-start(f32[2,32]{1,0:T(2,128)} %param.7) | copy-start | bytes 772
  13.3 7.6 %copy-start.6 = (f32[32]{0:T(128)S(1)}, f32[32]{0:T(128)}, u32[]{:S(2)}) copy-start(f32[32]{0:T(128)} %param.6) | copy-start | bytes 388
  13.3 7.9 %copy-start.4 = (s32[10,8]{0,1:T(8,128)S(1)}, s32[10,8]{0,1:T(8,128)}, u32[]{:S(2)}) copy-start(s32[10,8]{0,1:T(8,128)} %param.8) | copy-start | bytes 964
  13.3 103.5 %all-to-all-start = ((bf16[2,2,64,16,640]{4,2,1,0,3:T(8,128)(2,1)}), bf16[2,2,64,16,640]{4,2,1,0,3:T(8,128)(2,1)}, u32[]{:S(2)}, u32[]{:S(2)}) async-start(bf16[2,2,64,16,640]{4,2,1,0,3:T(8,128)(2,1)} %copy.34), calls=%async_computation | async-start | bytes 10485760 | tf_op jit(solution)/shard_map/all_to_all | solution.py:70
  20.9 269.9 %all-reduce.3.cloned.1.call-start = ((), (), s32[]{:S(2)}) async-start(), calls=%async_computation.1 | async-start | bytes 8388608 | tf_op jit(solution)/shard_map/psum | solution.py:88
  123.6 13.6 %copy-start.1 = (bf16[16,64,640]{2,1,0:T(8,128)(2,1)}, bf16[16,64,640]{2,1,0:T(8,128)(2,1)S(1)}, u32[]{:S(2)}) copy-start(bf16[16,64,640]{2,1,0:T(8,128)(2,1)S(1)} %copy.37) | copy-start | bytes 3932164
  125.5 10.1 %collective-permute-start = (bf16[1024,128]{1,0:T(8,128)(2,1)S(1)}, bf16[1024,128]{1,0:T(8,128)(2,1)S(1)}, u32[]{:S(2)}, u32[]{:S(2)}) collective-permute-start(bf16[1024,128]{1,0:T(8,128)(2,1)S(1)} %get-tuple-element.14), channel_id=1, source_target_pairs={{0,1},{1,2},{2,3},{3,4},{4,5},{5,6},{6,7},{7,8},{8,9},{9,10},{10,1... | collective-permute-start | bytes 786440 | tf_op jit(solution)/shard_map/ppermute | solution.py:18
  128.9 8.3 %collective-permute-start.1 = (bf16[1024,128]{1,0:T(8,128)(2,1)S(1)}, bf16[1024,128]{1,0:T(8,128)(2,1)S(1)}, u32[]{:S(2)}, u32[]{:S(2)}) collective-permute-start(bf16[1024,128]{1,0:T(8,128)(2,1)S(1)} %get-tuple-element.15), channel_id=1, source_target_pairs={{1,0},{2,1},{3,2},{4,3},{5,4},{6,5},{7,6},{8,7},{9,8},{10,9},{11,1... | collective-permute-start | bytes 786440 | tf_op jit(solution)/shard_map/ppermute | solution.py:21
  147.8 5.6 %copy-start.2 = (bf16[16,64,640]{2,1,0:T(8,128)(2,1)S(1)}, bf16[16,64,640]{2,1,0:T(8,128)(2,1)}, u32[]{:S(2)}) copy-start(bf16[16,64,640]{2,1,0:T(8,128)(2,1)} %copy-done.1) | copy-start | bytes 3932164
  155.2 1.2 copy-start.3
  159.6 246.8 %all-reduce.5.cloned.1.call-start = ((), (), s32[]{:S(2)}) async-start(), calls=%async_computation.2 | async-start | bytes 8388608 | tf_op jit(solution)/shard_map/psum | solution.py:87
Sparse Core Ops, SparseCore 0:
  159.7 131.0 all-reduce.2
  294.9 111.4 all-reduce.4
